TPU v7x, 32 devices: a whole 2x2x4 slice. The times are simulated.
32 devices in a mesh: groups: 2 (over x), tile: 16 (over z, y, core).
Axes of the slice: x: 2, y: 2, z: 4, core: 2. Of those that a mesh axis runs over, the one named last changes fastest.
Arguments:
- model_field: float32 [16, 524288], P(None, ('groups', 'tile')), parts along dimension 1, may hold values from -6 to 6
- direction: float32 [16, 524288], P(None, ('groups', 'tile')), parts along dimension 1, may hold values from -100 to 100
- old_grad: float32 [16, 524288], P(None, ('groups', 'tile')), parts along dimension 1, may hold values from -100 to 100
- residual: float32 [16, 65536], P(None, ('groups', 'tile')), parts along dimension 1, may hold values from -6 to 6
- block_pairs: int32 [256, 8], P(('groups', 'tile')), parts along dimension 0, may hold values from 0 to 159, as said below
- depth_band: int32 [524288], P(('groups', 'tile')), parts along dimension 0, may hold values from 0 to 15
- station_offsets: float32 [2, 65536], P(None, ('groups', 'tile')), parts along dimension 1, may hold values from -1.25 to 2.25, as said below
Outputs:
- new_model: float32 [16, 524288], P(None, ('groups', 'tile')), parts along dimension 1
- new_residual: float32 [16, 65536], P(None, ('groups', 'tile')), parts along dimension 1
- new_direction: float32 [16, 524288], P(None, ('groups', 'tile')), parts along dimension 1
There are 2 independent parts, one for each index of `groups`. A program takes and returns all parts, laid end to end along the dimension named above; each array names one. Nothing has to cross between parts.
Inputs may be any that keep to these rules, and one draw needn't show every extreme that they name: `block_pairs`: each row lists 8 different codes. `station_offsets`: row 1 (along) lies between 0 and 1.
All inputs are finite; a program needn't handle non-finite values.
Results may differ from a plain program's by a relative error of at most 0.0003.
Values sent between devices are 32-bit elements; how exact they have to be, the bound alone decides.
A program may use at most 128 MiB of HBM per device.

v0:
```python
import functools
import math

import jax
import jax.numpy as jnp
from jax import lax
from jax.experimental import pallas as pl
from jax.experimental.pallas import tpu as pltpu
from jax.sharding import PartitionSpec as P

CBLOCK = 512
SBLOCK = 256
REACH = 2
BANDS = 16
COL_SIDE = 32
DEPTH_RANGE = 2.0
DEPTH_SHIFT = 0.25
DAMPING = 1.0
GUARD = 1e-06

SPAN = 2 * REACH + 1
CHUNKS = 4
HOPS = tuple(r for r in range(-REACH, REACH + 1) if r != 0)
UNROLL = 8
KEPT = 88
STRIP = 64
STRETCH = 4.0
MESH = pl.DeviceIdType.MESH
F32 = jnp.float32
BF16 = jnp.bfloat16
VMEM_LIMIT = 4 * 1024 * 1024


def exists(me, r, n):
    return jnp.logical_and(me + r >= 0, me + r < n)


def split(x):
    high = x.astype(BF16)
    return high, (x - high.astype(F32)).astype(BF16)


def lane_sums(x):
    total = jnp.sum(x, axis=0, keepdims=True)
    out = total[:, 0:128]
    for k in range(1, x.shape[1] // 128):
        out = out + total[:, k * 128 : (k + 1) * 128]
    return out


def exchange_kernel(
    n, scale, blocks, dirn_hbm, pairs, band_hbm, offs_hbm,
    st_o, codes_o, v_o, f_o, z_o, norm_o,
    dirn, band, offs, in_sem, send_sem, recv_sem,
):
    me = lax.axis_index("tile")
    rows = pairs.shape[0]
    part = dirn.shape[1] // CHUNKS
    fetch_offs = pltpu.make_async_copy(offs_hbm, offs, in_sem.at[0])
    fetch_pairs = pltpu.make_async_copy(pairs, codes_o.at[REACH], in_sem.at[1])
    fetch_band = pltpu.make_async_copy(band_hbm, band, in_sem.at[2])
    fetch_dirn = [
        pltpu.make_async_copy(
            dirn_hbm.at[:, k * part : (k + 1) * part],
            dirn.at[:, k * part : (k + 1) * part],
            in_sem.at[3 + k],
        )
        for k in range(CHUNKS)
    ]
    for one in [fetch_offs, fetch_pairs, fetch_band] + fetch_dirn:
        one.start()
    barrier = pltpu.get_barrier_semaphore()
    for r in HOPS:
        @pl.when(exists(me, r, n))
        def _():
            pl.semaphore_signal(barrier, inc=1, device_id={"tile": me + r}, device_id_type=MESH)

    own = REACH * rows
    for r in HOPS:
        @pl.when(jnp.logical_not(exists(me, r, n)))
        def _():
            t = r + REACH
            st_o[:, t * rows : (t + 1) * rows] = jnp.zeros((2, rows, SBLOCK), F32)
            codes_o[t] = jnp.full(codes_o.shape[1:], -1, jnp.int32)
    fetch_offs.wait()
    for k in range(rows):
        for w in range(2):
            st_o[w, own + k : own + k + 1] = offs[w : w + 1, k * SBLOCK : (k + 1) * SBLOCK]
    fetch_pairs.wait()

    peers = sum(exists(me, r, n).astype(jnp.int32) for r in HOPS)
    pl.semaphore_wait(barrier, peers)

    def copies(q, r):
        t = REACH - r
        made = []
        for which, (src, dst) in enumerate((
            (codes_o.at[REACH], codes_o.at[t]),
            (st_o.at[:, pl.ds(own, rows)], st_o.at[:, pl.ds(t * rows, rows)]),
        )):
            made.append(pltpu.make_async_remote_copy(
                src_ref=src, dst_ref=dst, send_sem=send_sem.at[which, q],
                recv_sem=recv_sem.at[which, q], device_id={"tile": me + r}, device_id_type=MESH,
            ))
        return made

    for q, r in enumerate(HOPS):
        @pl.when(exists(me, r, n))
        def _():
            for one in copies(q, r):
                one.start()

    fetch_band.wait()
    depth = (band[...].astype(F32) + 0.5) * (DEPTH_RANGE / BANDS)
    shifted = depth + DEPTH_SHIFT
    f_o[...] = (scale * STRETCH**3) * depth * (shifted * jnp.sqrt(shifted))
    q = lax.bitwise_and(lax.broadcasted_iota(jnp.int32, z_o.shape, 0), 3).astype(F32)
    z_o[...] = (STRETCH * STRETCH) * (depth * depth) + 0.25 * (q * q)

    def block(b, total):
        for q in range(CBLOCK // 128):
            lanes = pl.ds(pl.multiple_of(b * CBLOCK + q * 128, 128), 128)
            values = dirn[:, lanes]
            high, low = split(f_o[pl.ds(b * (CBLOCK // 128) + q, 1), :] * values)
            v_o[b, 0:16, q * 128 : (q + 1) * 128] = high
            v_o[b, 16:32, q * 128 : (q + 1) * 128] = low
            total = total + values * values
        return total

    total = jnp.zeros((dirn.shape[0], 128), F32)
    for k in range(CHUNKS):
        fetch_dirn[k].wait()
        total = lax.fori_loop(k * blocks // CHUNKS, (k + 1) * blocks // CHUNKS, block, total)
    norm_o[...] = jnp.broadcast_to(lane_sums(total), norm_o.shape)

    for q, r in enumerate(HOPS):
        @pl.when(exists(me, r, n))
        def _():
            for one in copies(q, r):
                one.wait_send()

        @pl.when(exists(me, -r, n))
        def _():
            for one in copies(q, r):
                one.wait_recv()


def fill_block(entry, slots, places, z, dst):
    j = lax.shift_right_logical(entry, 5)
    b = lax.bitwise_and(entry, 31)
    at = jnp.minimum(j, slots - 1)
    parity = lax.bitwise_and(b, 1).astype(F32)
    lane = lax.broadcasted_iota(jnp.int32, (8, 128), 1)
    unit = STRETCH / COL_SIDE
    cell_across = (lax.rem(lane, COL_SIDE).astype(F32) + 0.5) * unit
    cell_along = (lax.div(lane, COL_SIDE).astype(F32) + 0.5) * unit + (0.5 * STRETCH) * parity
    cell_across = jnp.concatenate([cell_across] * (STRIP // 8), axis=0)
    cell_along = jnp.concatenate([cell_along] * (STRIP // 8), axis=0)
    which = jnp.full((STRIP, 128), at, jnp.int32)
    deeps = [
        jnp.broadcast_to(z[pl.ds(b * (CBLOCK // 128) + q, 1), :], (8, 128))
        for q in range(CBLOCK // 128)
    ]
    for k in range(SBLOCK // STRIP):
        rows = slice(k * STRIP, (k + 1) * STRIP)
        across = jnp.take_along_axis(places[0, rows, :], which, axis=1) - cell_across
        along = jnp.take_along_axis(places[1, rows, :], which, axis=1) - cell_along
        flat = across * across + along * along
        for q in range(CBLOCK // 128):
            if q > 0:
                flat = flat - along
            inverse = lax.rsqrt(flat + jnp.concatenate([deeps[q]] * (STRIP // 8), axis=0))
            high, low = split(inverse * inverse * inverse)
            dst[0, q, rows, :] = high
            dst[1, q, rows, :] = low
    return j, b


def block_part(block, w):
    return jnp.concatenate([block[w, q] for q in range(CBLOCK // 128)], axis=1)


def forward_kernel(codes, st, z, v, img, pair_list, count, places, *rest):
    kept, spare = rest[:UNROLL], rest[UNROLL]
    slots = st.shape[1]
    pad = jnp.zeros((128 - slots, SBLOCK), F32)
    shift = lax.broadcasted_iota(jnp.int32, (slots, SBLOCK), 0) // codes.shape[1] - REACH
    places[0] = jnp.concatenate([STRETCH * (st[0] + shift.astype(F32)), pad], axis=0).T
    places[1] = jnp.concatenate([STRETCH * st[1], pad], axis=0).T
    rows = codes.shape[1]
    img[...] = jnp.zeros(img.shape, F32)
    filled = jnp.int32(0)
    for t in range(SPAN):
        def pick(row, filled):
            for p in range(codes.shape[2]):
                code = codes[t, row, p]
                pair_list[filled] = (t * rows + row) * 32 + lax.bitwise_and(code, 31)
                hit = lax.shift_right_arithmetic(code, 5) == SPAN - 1 - t
                filled = filled + hit.astype(jnp.int32)
            return filled
        filled = lax.fori_loop(0, rows, pick, filled)
    for u in range(UNROLL):
        pair_list[filled + u] = SPAN * rows * 32
    steps = (filled + (UNROLL - 1)) // UNROLL
    count[0] = steps
    count[1] = jnp.minimum(steps, KEPT // UNROLL)

    def step(keep, i, carry):
        for u in range(UNROLL):
            block = kept[u].at[i] if keep else spare
            j, b = fill_block(pair_list[i * UNROLL + u], slots, places, z, block)
            out = jnp.zeros((32, SBLOCK), F32)
            for w in range(2):
                out = out + lax.dot_general(
                    v[b], block_part(block, w), (((1,), (1,)), ((), ())), preferred_element_type=F32
                )
            img[j] += out[0:16] + out[16:32]
        return carry

    lax.fori_loop(0, count[1], functools.partial(step, True), 0)
    lax.fori_loop(count[1], steps, functools.partial(step, False), 0)


def all_sum(n, me, mine, landing, send_sem, recv_sem, start, finish):
    def made(k):
        return pltpu.make_async_remote_copy(
            src_ref=mine, dst_ref=landing.at[k], send_sem=send_sem.at[k], recv_sem=recv_sem.at[k],
            device_id={"tile": lax.rem(me + k, n)}, device_id_type=MESH,
        )
    if start:
        def go(k, c):
            made(k).start()
            return c
        lax.fori_loop(1, n, go, 0)
    if finish:
        def done(k, c):
            made(k).wait()
            return c
        lax.fori_loop(1, n, done, 0)


def greet(n, me):
    barrier = pltpu.get_barrier_semaphore()

    def one(k, c):
        pl.semaphore_signal(
            barrier, inc=1, device_id={"tile": lax.rem(me + k, n)}, device_id_type=MESH
        )
        return c
    lax.fori_loop(1, n, one, 0)


def greeted(n):
    pl.semaphore_wait(pltpu.get_barrier_semaphore(), n - 1)


def image_kernel(
    n, rows, img, res_hbm, norm, old_hbm, newres_o, scal_o,
    res, old, in_sem, transit, joined, part_rx, norm_tx, norm_rx, send_sem, recv_sem, nsend_sem, nrecv_sem,
):
    me = lax.axis_index("tile")
    greet(n, me)
    fetch_old = pltpu.make_async_copy(old_hbm, old, in_sem.at[0])
    fetch_res = pltpu.make_async_copy(res_hbm, res, in_sem.at[1])
    fetch_old.start()
    fetch_res.start()
    greeted(n)
    s = 1 - 2 * lax.rem(me, 2)
    outward = exists(me, -2 * s, n)
    inward = exists(me, 2 * s, n)

    def slab(ref, r):
        return ref.at[pl.ds((REACH + r) * rows, rows)]

    def copy(number, src, dst, to):
        return pltpu.make_async_remote_copy(
            src_ref=src, dst_ref=dst, send_sem=send_sem.at[number],
            recv_sem=recv_sem.at[number], device_id={"tile": to}, device_id_type=MESH,
        )

    to_join = copy(0, slab(img, 2 * s), transit, me + s)
    to_sibling = copy(1, slab(img, s), part_rx.at[0], me + s)
    to_far = copy(2, slab(img, -2 * s), part_rx.at[1], me - 2 * s)
    to_near = copy(3, joined, part_rx.at[2], me - s)
    own = slab(newres_o, 0)
    give_near = copy(4, own, slab(newres_o, s), me - s)
    give_far = copy(5, own, slab(newres_o, -2 * s), me + 2 * s)
    give_sibling = copy(6, own, slab(newres_o, -s), me + s)
    pass_on = copy(7, slab(newres_o, -s), slab(newres_o, -2 * s), me + s)

    @pl.when(inward)
    def _():
        to_join.start()

    @pl.when(outward)
    def _():
        to_far.start()
    to_sibling.start()

    def squares(k, total):
        values = old[:, pl.ds(pl.multiple_of(k * 512, 512), 512)]
        return total + values * values

    fetch_old.wait()
    fetch_res.wait()
    before = lax.fori_loop(0, old.shape[1] // 512, squares, jnp.zeros((old.shape[0], 512), F32))
    lane = lax.broadcasted_iota(jnp.int32, (1, 128), 1)
    gamma_part = jnp.sum(lane_sums(before), axis=1, keepdims=True)
    norm_part = DAMPING * jnp.sum(norm[0:1, :], axis=1, keepdims=True)
    known = jnp.where(lane == 0, gamma_part, jnp.where(lane == 1, norm_part, 0.0))

    @pl.when(outward)
    def _():
        to_join.wait_recv()
        joined[...] = transit[...] + img[pl.ds((REACH - s) * rows, rows)]
        to_near.start()

    to_sibling.wait_recv()
    here = REACH * rows
    newres_o[here : here + rows] = img[here : here + rows] + part_rx[0]

    @pl.when(inward)
    def _():
        to_far.wait_recv()
        newres_o[here : here + rows] += part_rx[1]

    @pl.when(outward)
    def _():
        to_near.wait_recv()
        newres_o[here : here + rows] += part_rx[2]

    image = newres_o[here : here + rows]
    squared = lane_sums(jnp.sum(image * image, axis=0))
    folded = squared + jnp.where(lane == 1, 0.0, pltpu.roll(jnp.where(lane < 2, squared, 0.0), 2, 1))
    norm_tx[...] = jnp.where(lane < 2, known, folded)
    all_sum(n, me, norm_tx, norm_rx, nsend_sem, nrecv_sem, True, True)
    norm_rx[0] = norm_tx[...]
    totals = jnp.sum(norm_rx[...], axis=0)
    gamma_old = jnp.sum(jnp.where(lane == 0, totals, 0.0), axis=1, keepdims=True)
    curvature = jnp.sum(jnp.where(lane == 0, 0.0, totals), axis=1, keepdims=True)
    length = gamma_old / (curvature + GUARD)
    scal_o[...] = jnp.concatenate(
        [jnp.broadcast_to(length, (4, 128)), jnp.broadcast_to(gamma_old, (4, 128))], axis=0
    )
    for k in range(rows):
        newres_o[here + k] = res[:, k * SBLOCK : (k + 1) * SBLOCK] - length * newres_o[here + k]

    @pl.when(outward)
    def _():
        give_near.start()

    @pl.when(inward)
    def _():
        give_far.start()
    give_sibling.start()

    @pl.when(outward)
    def _():
        give_near.wait_recv()
        pass_on.start()
        to_far.wait_send()
        to_near.wait_send()
        give_far.wait_recv()
        give_near.wait_send()
        pass_on.wait_send()

    @pl.when(inward)
    def _():
        to_join.wait_send()
        give_far.wait_send()
        pass_on.wait_recv()
    to_sibling.wait_send()
    give_sibling.wait()


def adjoint_kernel(pair_list, count, places, z, newres, scal, model_in, dirn_in, *rest):
    kept = rest[:UNROLL]
    model_hbm, model_o, acc, res_o, dirn, parts, spare, in_sem, out_sem = rest[UNROLL:]
    slots = newres.shape[0]
    rows = slots // SPAN
    fetch_model = pltpu.make_async_copy(model_in, model_o, in_sem.at[0])
    fetch_dirn = pltpu.make_async_copy(dirn_in, dirn, in_sem.at[1])
    fetch_model.start()
    fetch_dirn.start()
    for k in range(rows):
        res_o[:, k * SBLOCK : (k + 1) * SBLOCK] = newres[REACH * rows + k]

    def cut(k, c):
        high, low = split(newres[k])
        parts[k, 0:16, :] = high
        parts[k, 16:32, :] = low
        return c
    lax.fori_loop(0, slots, cut, 0)
    parts[slots] = jnp.zeros((32, SBLOCK), BF16)
    acc[...] = jnp.zeros(acc.shape, F32)

    def add_pair(j, b, block):
        out = jnp.zeros((32, CBLOCK), F32)
        for w in range(2):
            out = out + jnp.dot(parts[j], block_part(block, w), preferred_element_type=F32)
        acc[b] += out[0:16] + out[16:32]

    def reread(i, carry):
        for u in range(UNROLL):
            entry = pair_list[i * UNROLL + u]
            add_pair(lax.shift_right_logical(entry, 5), lax.bitwise_and(entry, 31), kept[u].at[i])
        return carry

    def rebuild(i, carry):
        for u in range(UNROLL):
            j, b = fill_block(pair_list[i * UNROLL + u], slots, places, z, spare)
            add_pair(j, b, spare)
        return carry

    first = jnp.minimum(count[1], 1)
    lax.fori_loop(0, first, reread, 0)
    fetch_model.wait()
    fetch_dirn.wait()
    length = scal[0:1, 0:1]

    def update(b, c):
        lanes = pl.ds(pl.multiple_of(b * CBLOCK, CBLOCK), CBLOCK)
        model_o[:, lanes] = model_o[:, lanes] + length * dirn[:, lanes]
        return c
    lax.fori_loop(0, acc.shape[0], update, 0)
    leave = pltpu.make_async_copy(model_o, model_hbm, out_sem)
    leave.start()
    lax.fori_loop(first, count[1], reread, 0)
    lax.fori_loop(count[1], count[0], rebuild, 0)
    leave.wait()


def gamma_kernel(n, acc, model, f, scal, grad_o, ratio_o, mine, landing, send_sem, recv_sem):
    me = lax.axis_index("tile")
    greet(n, me)

    def finish(b, total):
        lanes = pl.ds(pl.multiple_of(b * CBLOCK, CBLOCK), CBLOCK)
        factor = jnp.concatenate(
            [f[pl.ds(b * (CBLOCK // 128) + q, 1), :] for q in range(CBLOCK // 128)], axis=1
        )
        gradient = factor * acc[b] - DAMPING * model[:, lanes]
        grad_o[:, lanes] = gradient
        return total + gradient * gradient

    total = lax.fori_loop(0, acc.shape[0], finish, jnp.zeros((model.shape[0], CBLOCK), F32))
    mine[...] = lane_sums(total)
    greeted(n)
    all_sum(n, me, mine, landing, send_sem, recv_sem, True, True)
    landing[0] = mine[...]
    total = jnp.sum(jnp.sum(landing[...], axis=0), axis=1, keepdims=True)
    ratio_o[...] = total / (scal[4:5, 0:1] + GUARD)


def shards(model_field, direction, old_grad, residual, block_pairs, depth_band, station_offsets):
    n = lax.axis_size("tile")
    epochs, cells = model_field.shape
    stations = residual.shape[1]
    rows = block_pairs.shape[0]
    pairs = block_pairs.shape[1]
    blocks = cells // CBLOCK
    scale = 2.0 / math.sqrt(cells)
    vmem = pl.BlockSpec(memory_space=pltpu.VMEM)
    smem = pl.BlockSpec(memory_space=pltpu.SMEM)
    hbm = pl.BlockSpec(memory_space=pltpu.HBM)
    shape = jax.ShapeDtypeStruct
    slots = SPAN * rows
    one_block = (2, CBLOCK // 128, SBLOCK, 128)
    dma = pltpu.SemaphoreType.DMA

    def in_hbm(one):
        return pltpu.with_memory_space_constraint(one, pltpu.HBM)

    def params(number=None):
        if number is None:
            return pltpu.CompilerParams(vmem_limit_bytes=VMEM_LIMIT)
        return pltpu.CompilerParams(
            vmem_limit_bytes=VMEM_LIMIT, collective_id=number, has_side_effects=True
        )

    st, codes, v, f, z, norm = pl.pallas_call(
        functools.partial(exchange_kernel, n, scale, blocks),
        out_shape=(
            shape((2, slots, SBLOCK), F32),
            shape((SPAN, rows, pairs), jnp.int32),
            shape((blocks, 2 * epochs, CBLOCK), BF16),
            shape((cells // 128, 128), F32),
            shape((cells // 128, 128), F32),
            shape((8, 128), F32),
        ),
        in_specs=[hbm] * 4,
        out_specs=(vmem,) * 6,
        scratch_shapes=[
            pltpu.VMEM((epochs, cells), F32),
            pltpu.VMEM((cells // 128, 128), jnp.int32),
            pltpu.VMEM((2, stations), F32),
            dma((3 + CHUNKS,)),
            dma((2, len(HOPS))),
            dma((2, len(HOPS))),
        ],
        compiler_params=params(0),
        name="exchange",
    )(
        in_hbm(direction), in_hbm(block_pairs),
        in_hbm(depth_band.reshape(cells // 128, 128)), in_hbm(station_offsets),
    )

    img, pair_list, count, places, *kept = pl.pallas_call(
        forward_kernel,
        out_shape=(
            shape((slots + 1, epochs, SBLOCK), F32),
            shape((slots * pairs + UNROLL,), jnp.int32),
            shape((2,), jnp.int32),
            shape((2, SBLOCK, 128), F32),
        ) + (pltpu.VMEM((KEPT // UNROLL,) + one_block, BF16),) * UNROLL,
        in_specs=[smem, vmem, vmem, vmem],
        out_specs=(vmem, smem, smem) + (vmem,) * (1 + UNROLL),
        scratch_shapes=[pltpu.VMEM(one_block, BF16)],
        compiler_params=params(),
        name="forward",
    )(codes, st, z, v)

    kept = [pltpu.with_memory_space_constraint(one, pltpu.VMEM) for one in kept]
    newres, scal = pl.pallas_call(
        functools.partial(image_kernel, n, rows),
        out_shape=(shape((slots, epochs, SBLOCK), F32), shape((8, 128), F32)),
        in_specs=[vmem, hbm, vmem, hbm],
        out_specs=(vmem,) * 2,
        scratch_shapes=[
            pltpu.VMEM((epochs, stations), F32),
            pltpu.VMEM((epochs, cells), F32),
            dma((2,)),
            pltpu.VMEM((rows, epochs, SBLOCK), F32),
            pltpu.VMEM((rows, epochs, SBLOCK), F32),
            pltpu.VMEM((3, rows, epochs, SBLOCK), F32),
            pltpu.VMEM((1, 128), F32),
            pltpu.VMEM((n, 1, 128), F32),
            dma((8,)),
            dma((8,)),
            dma((n,)),
            dma((n,)),
        ],
        compiler_params=params(1),
        name="images",
    )(img, in_hbm(residual), norm, in_hbm(old_grad))

    new_model, model_kept, acc, new_residual = pl.pallas_call(
        adjoint_kernel,
        out_shape=(
            shape((epochs, cells), F32),
            shape((epochs, cells), F32),
            shape((blocks, epochs, CBLOCK), F32),
            shape((epochs, stations), F32),
        ),
        in_specs=[smem, smem] + [vmem] * 4 + [hbm] * 2 + [vmem] * UNROLL,
        out_specs=(hbm,) + (vmem,) * 3,
        scratch_shapes=[
            pltpu.VMEM((epochs, cells), F32),
            pltpu.VMEM((slots + 1, 2 * epochs, SBLOCK), BF16),
            pltpu.VMEM(one_block, BF16),
            dma((2,)),
            dma(()),
        ],
        compiler_params=params(),
        name="adjoint",
    )(
        pair_list, count, places, z, newres, scal, in_hbm(model_field), in_hbm(direction), *kept
    )

    gradient, ratio = pl.pallas_call(
        functools.partial(gamma_kernel, n),
        out_shape=(shape((epochs, cells), F32), shape((1, 1), F32)),
        in_specs=[vmem] * 4,
        out_specs=(vmem,) * 2,
        scratch_shapes=[
            pltpu.VMEM((1, 128), F32), pltpu.VMEM((n, 1, 128), F32), dma((n,)), dma((n,)),
        ],
        compiler_params=params(2),
        name="gamma",
    )(acc, model_kept, f, scal)
    new_direction = gradient + ratio.reshape(()) * direction
    return (new_model, new_residual, new_direction)


def solution(mesh):
    both = ("groups", "tile")
    wide = P(None, both)
    return jax.shard_map(
        shards,
        mesh=mesh,
        in_specs=(wide, wide, wide, wide, P(both, None), P(both), wide),
        out_specs=(wide, wide, wide),
        check_vma=False,
    )
```

profile of v0, /device:TPU:0, one launch (start us, length us, event | category | flops | bytes accessed | tf_op | source)
XLA Modules:
  0.0 70.1 jit_solution(3915118560354691397)
XLA Ops:
  0.6 6.5 %exchange.1 = (f32[2,40,256]{2,1,0:T(8,128)S(1)}, s32[5,8,8]{2,1,0:T(8,128)S(1)}, bf16[32,32,512]{2,1,0:T(8,128)(2,1)S(1)}, f32[128,128]{1,0:T(8,128)S(1)}, f32[...) custom-call(f32[16,16384]{1,0:T(8,128)} %dirn_in.1, s32[8,8]{1,0:T(8,128)} %pairs.1, s32[128,128]{1,0:T(8,128)} %bitcast.2, ...), custom_call_target="tpu_custom_call" | custom-call | tf_op jit(solution)/shard_map/exchange/pallas_call | solution.py:481
  7.1 11.6 %forward.1 = (f32[41,16,256]{2,1,0:T(8,128)S(1)}, s32[328]{0:T(512)S(1)}, s32[2]{0:T(128)S(1)}, f32[2,256,128]{2,1,0:T(8,128)S(1)}, bf16[11,2,4,256,128]{4,3,2,1...) custom-call(s32[5,8,8]{2,1,0:T(8,128)S(1)} %get-tuple-element.29.cod, ...), custom_call_target="tpu_custom_call" | custom-call | tf_op jit(solution)/shard_map/forward/pallas_call | solution.py:508
  18.8 29.4 %images.1 = (f32[40,16,256]{2,1,0:T(8,128)S(1)}, f32[8,128]{1,0:T(8,128)S(1)}) custom-call(f32[41,16,256]{2,1,0:T(8,128)S(1)} %get-tuple-element.36.img, f32[16,2048]{1,0:T(8,128)} %res_hbm.1, f32[8,128]{1,0:T(8,128)S(1)} %get-tuple-element.37.norm, f32[16,16384]{1,0:T(8,128)} %old_hbm.1), custom_call_target="tpu_custom_call" | custom-call | tf_op jit(solution)/shard_map/images/pallas_call | solution.py:524
  48.2 0.0 copy-start
  48.2 7.2 %adjoint.1 = (f32[16,16384]{1,0:T(8,128)}, f32[16,16384]{1,0:T(8,128)S(1)}, f32[32,16,512]{2,1,0:T(8,128)S(1)}, f32[16,2048]{1,0:T(8,128)}) custom-call(s32[328]{0:T(512)S(1)} %get-tuple-element.33.pair_list, s32[2]{0:T(128)S(1)} %get-tuple-element.34.count, f32[2,256,128]{2,1,0:T(8,128)S(1)} %get-tuple-element.35.places, ...), custom_call_target="tpu_custom_call" | custom-call | tf_op jit(solution)/shard_map/adjoint/pallas_call | solution.py:547
  55.3 13.0 %gamma.1 = (f32[16,16384]{1,0:T(8,128)S(1)}, f32[1,1]{1,0:T(1,128)}) custom-call(f32[32,16,512]{2,1,0:T(8,128)S(1)} %get-tuple-element.50.acc, f32[16,16384]{1,0:T(8,128)S(1)} %get-tuple-element.51.model, f32[128,128]{1,0:T(8,128)S(1)} %get-tuple-element.52.f, f32[8,128]{1,0:T(8,128)S(1)} %get-tuple-element.39.scal), custom_call_target="tpu_custom_call" | custom-call | tf_op jit(solution)/shard_map/gamma/pallas_call | solution.py:570
  68.3 0.0 copy-done
  68.4 1.7 %multiply_add_fusion = f32[16,16384]{1,0:T(8,128)} fusion(f32[16,16384]{1,0:T(8,128)S(1)} %get-tuple-element.53, f32[16,16384]{1,0:T(8,128)S(1)} %copy-done, f32[]{:T(128)} %bitcast.1), kind=kLoop, calls=%fused_computation | loop fusion | flops 524288 | bytes 3145732 | tf_op jit(solution)/shard_map/add | solution.py:581
Async XLA Ops:
  48.2 20.2 %copy-start = (f32[16,16384]{1,0:T(8,128)S(1)}, f32[16,16384]{1,0:T(8,128)}, u32[]{:S(2)}) copy-start(f32[16,16384]{1,0:T(8,128)} %dirn_in.1) | copy-start | bytes 3145732
where the time goes:
time: 69.9 us; the launch traced here: 70.1 us
  Pallas kernels  67.7 us (97%)
  other arithmetic  1.72 us (2%)
    pallas_call x1, Pallas kernels, shards(): pl.pallas_call(functools.partial(image_kernel, n, rows), out_shape=(shape...  29.4 us
    pallas_call x1, Pallas kernels, shards(): pl.pallas_call(functools.partial(gamma_kernel, n), out_shape=(shape((epoc...  13 us
    pallas_call x1, Pallas kernels, shards(): pl.pallas_call(forward_kernel, out_shape=(shape((slots + 1, epochs, SBLOC...  11.6 us
    pallas_call x1, Pallas kernels, shards(): pl.pallas_call(adjoint_kernel, out_shape=(shape((epochs, cells), F32), sh...  7.17 us
    pallas_call x1, Pallas kernels, shards(): pl.pallas_call(functools.partial(exchange_kernel, n, scale, blocks), out_...  6.5 us
    add x1, other arithmetic, shards(): new_direction = gradient + ratio.reshape(()) * direction  1.72 us

commit v1 on v0

--- a/solution.py
+++ b/solution.py
@@ -50,7 +50,7 @@
 
 def exchange_kernel(
     n, scale, blocks, dirn_hbm, pairs, band_hbm, offs_hbm,
-    st_o, codes_o, v_o, f_o, z_o, norm_o,
+    st_o, entries_o, v_o, f_o, z_o, norm_o, codes_o,
     dirn, band, offs, in_sem, send_sem, recv_sem,
 ):
     me = lax.axis_index("tile")
@@ -143,6 +143,12 @@
         def _():
             for one in copies(q, r):
                 one.wait_recv()
+
+    codes = codes_o[...]
+    slot = lax.broadcasted_iota(jnp.int32, codes.shape, 0)
+    hit = lax.shift_right_arithmetic(codes, 5) == SPAN - 1 - slot
+    slot = slot * rows + lax.broadcasted_iota(jnp.int32, codes.shape, 1)
+    entries_o[...] = jnp.where(hit, slot * 32 + lax.bitwise_and(codes, 31), -1)
 
 
 def fill_block(entry, slots, places, z, dst):
@@ -180,45 +186,66 @@
     return jnp.concatenate([block[w, q] for q in range(CBLOCK // 128)], axis=1)
 
 
-def forward_kernel(codes, st, z, v, img, pair_list, count, places, *rest):
+def forward_kernel(entries, st, z, v, img, pair_list, count, places, *rest):
     kept, spare = rest[:UNROLL], rest[UNROLL]
     slots = st.shape[1]
     pad = jnp.zeros((128 - slots, SBLOCK), F32)
-    shift = lax.broadcasted_iota(jnp.int32, (slots, SBLOCK), 0) // codes.shape[1] - REACH
+    shift = lax.broadcasted_iota(jnp.int32, (slots, SBLOCK), 0) // entries.shape[1] - REACH
     places[0] = jnp.concatenate([STRETCH * (st[0] + shift.astype(F32)), pad], axis=0).T
     places[1] = jnp.concatenate([STRETCH * st[1], pad], axis=0).T
-    rows = codes.shape[1]
+    rows = entries.shape[1]
     img[...] = jnp.zeros(img.shape, F32)
-    filled = jnp.int32(0)
+    nothing = SPAN * rows * 32
+    pair_list[UNROLL - 1] = nothing
+    filled = jnp.int32(UNROLL)
     for t in range(SPAN):
         def pick(row, filled):
-            for p in range(codes.shape[2]):
-                code = codes[t, row, p]
-                pair_list[filled] = (t * rows + row) * 32 + lax.bitwise_and(code, 31)
-                hit = lax.shift_right_arithmetic(code, 5) == SPAN - 1 - t
-                filled = filled + hit.astype(jnp.int32)
+            for p in range(entries.shape[2]):
+                entry = entries[t, row, p]
+                pair_list[filled] = entry
+                filled = filled + (entry >= 0).astype(jnp.int32)
             return filled
         filled = lax.fori_loop(0, rows, pick, filled)
     for u in range(UNROLL):
-        pair_list[filled + u] = SPAN * rows * 32
-    steps = (filled + (UNROLL - 1)) // UNROLL
+        pair_list[filled + u] = nothing
+    steps = (filled - 1) // UNROLL
+    held = jnp.minimum(steps, KEPT // UNROLL)
     count[0] = steps
-    count[1] = jnp.minimum(steps, KEPT // UNROLL)
-
-    def step(keep, i, carry):
+    count[1] = held
+
+    def multiply(entry, block):
+        j = lax.shift_right_logical(entry, 5)
+        b = lax.bitwise_and(entry, 31)
+        out = jnp.zeros((32, SBLOCK), F32)
+        for w in range(2):
+            out = out + lax.dot_general(
+                v[b], block_part(block, w), (((1,), (1,)), ((), ())), preferred_element_type=F32
+            )
+        img[j] += out[0:16] + out[16:32]
+
+    last = UNROLL - 1
+    kept[last][0] = jnp.zeros(kept[last].shape[1:], BF16)
+
+    def step(i, carry):
+        at = (i + 1) * UNROLL
         for u in range(UNROLL):
-            block = kept[u].at[i] if keep else spare
-            j, b = fill_block(pair_list[i * UNROLL + u], slots, places, z, block)
-            out = jnp.zeros((32, SBLOCK), F32)
-            for w in range(2):
-                out = out + lax.dot_general(
-                    v[b], block_part(block, w), (((1,), (1,)), ((), ())), preferred_element_type=F32
-                )
-            img[j] += out[0:16] + out[16:32]
+            fill_block(pair_list[at + u], slots, places, z, kept[u].at[i])
+            if u == 0:
+                multiply(pair_list[at - 1], kept[last].at[jnp.maximum(i - 1, 0)])
+            else:
+                multiply(pair_list[at + u - 1], kept[u - 1].at[i])
         return carry
 
-    lax.fori_loop(0, count[1], functools.partial(step, True), 0)
-    lax.fori_loop(count[1], steps, functools.partial(step, False), 0)
+    def step_over(i, carry):
+        for u in range(UNROLL):
+            entry = pair_list[(i + 1) * UNROLL + u]
+            fill_block(entry, slots, places, z, spare)
+            multiply(entry, spare)
+        return carry
+
+    lax.fori_loop(0, held, step, 0)
+    multiply(pair_list[held * UNROLL + last], kept[last].at[jnp.maximum(held - 1, 0)])
+    lax.fori_loop(held, steps, step_over, 0)
 
 
 def all_sum(n, me, mine, landing, send_sem, recv_sem, start, finish):
@@ -402,13 +429,13 @@
 
     def reread(i, carry):
         for u in range(UNROLL):
-            entry = pair_list[i * UNROLL + u]
+            entry = pair_list[(i + 1) * UNROLL + u]
             add_pair(lax.shift_right_logical(entry, 5), lax.bitwise_and(entry, 31), kept[u].at[i])
         return carry
 
     def rebuild(i, carry):
         for u in range(UNROLL):
-            j, b = fill_block(pair_list[i * UNROLL + u], slots, places, z, spare)
+            j, b = fill_block(pair_list[(i + 1) * UNROLL + u], slots, places, z, spare)
             add_pair(j, b, spare)
         return carry
 
@@ -478,7 +505,7 @@
             vmem_limit_bytes=VMEM_LIMIT, collective_id=number, has_side_effects=True
         )
 
-    st, codes, v, f, z, norm = pl.pallas_call(
+    st, entries, v, f, z, norm = pl.pallas_call(
         functools.partial(exchange_kernel, n, scale, blocks),
         out_shape=(
             shape((2, slots, SBLOCK), F32),
@@ -491,6 +518,7 @@
         in_specs=[hbm] * 4,
         out_specs=(vmem,) * 6,
         scratch_shapes=[
+            pltpu.VMEM((SPAN, rows, pairs), jnp.int32),
             pltpu.VMEM((epochs, cells), F32),
             pltpu.VMEM((cells // 128, 128), jnp.int32),
             pltpu.VMEM((2, stations), F32),
@@ -509,7 +537,7 @@
         forward_kernel,
         out_shape=(
             shape((slots + 1, epochs, SBLOCK), F32),
-            shape((slots * pairs + UNROLL,), jnp.int32),
+            shape((slots * pairs + 2 * UNROLL,), jnp.int32),
             shape((2,), jnp.int32),
             shape((2, SBLOCK, 128), F32),
         ) + (pltpu.VMEM((KEPT // UNROLL,) + one_block, BF16),) * UNROLL,
@@ -518,7 +546,7 @@
         scratch_shapes=[pltpu.VMEM(one_block, BF16)],
         compiler_params=params(),
         name="forward",
-    )(codes, st, z, v)
+    )(entries, st, z, v)
 
     kept = [pltpu.with_memory_space_constraint(one, pltpu.VMEM) for one in kept]
     newres, scal = pl.pallas_call(

time: 69.9 us -> 69 us (0.987)
    pallas_call x1, Pallas kernels: 11.6 us -> 10.8 us  [shards(): pl.pallas_call(forward_kernel, out_shape=(shape((slots + 1, epochs, SBLOC...]
where the time goes in v1:
time: 69 us; the launch traced here: 69.7 us
  Pallas kernels  67.3 us (98%)
  other arithmetic  1.72 us (2%)
    pallas_call x1, Pallas kernels, shards(): pl.pallas_call(functools.partial(image_kernel, n, rows), out_shape=(shape...  29.2 us
    pallas_call x1, Pallas kernels, shards(): pl.pallas_call(functools.partial(gamma_kernel, n), out_shape=(shape((epoc...  13.6 us
    pallas_call x1, Pallas kernels, shards(): pl.pallas_call(forward_kernel, out_shape=(shape((slots + 1, epochs, SBLOC...  10.8 us
    pallas_call x1, Pallas kernels, shards(): pl.pallas_call(adjoint_kernel, out_shape=(shape((epochs, cells), F32), sh...  7.17 us
    pallas_call x1, Pallas kernels, shards(): pl.pallas_call(functools.partial(exchange_kernel, n, scale, blocks), out_...  6.51 us
    add x1, other arithmetic, shards(): new_direction = gradient + ratio.reshape(()) * direction  1.72 us

profile of v1, /device:TPU:0, one launch (start us, length us, event | category | flops | bytes accessed | tf_op | source)
XLA Modules:
  0.0 69.7 jit_solution(6649104261196752965)
XLA Ops:
  0.6 6.5 %exchange.1 = (f32[2,40,256]{2,1,0:T(8,128)S(1)}, s32[5,8,8]{2,1,0:T(8,128)S(1)}, bf16[32,32,512]{2,1,0:T(8,128)(2,1)S(1)}, f32[128,128]{1,0:T(8,128)S(1)}, f32[...) custom-call(f32[16,16384]{1,0:T(8,128)} %dirn_in.1, s32[8,8]{1,0:T(8,128)} %pairs.1, s32[128,128]{1,0:T(8,128)} %bitcast.2, ...), custom_call_target="tpu_custom_call" | custom-call | tf_op jit(solution)/shard_map/exchange/pallas_call | solution.py:508
  7.1 10.8 %forward.1 = (f32[41,16,256]{2,1,0:T(8,128)S(1)}, s32[336]{0:T(512)S(1)}, s32[2]{0:T(128)S(1)}, f32[2,256,128]{2,1,0:T(8,128)S(1)}, bf16[11,2,4,256,128]{4,3,2,1...) custom-call(s32[5,8,8]{2,1,0:T(8,128)S(1)} %get-tuple-element.29.ent, ...), custom_call_target="tpu_custom_call" | custom-call | tf_op jit(solution)/shard_map/forward/pallas_call | solution.py:536
  18.0 29.2 %images.1 = (f32[40,16,256]{2,1,0:T(8,128)S(1)}, f32[8,128]{1,0:T(8,128)S(1)}) custom-call(f32[41,16,256]{2,1,0:T(8,128)S(1)} %get-tuple-element.36.img, f32[16,2048]{1,0:T(8,128)} %res_hbm.1, f32[8,128]{1,0:T(8,128)S(1)} %get-tuple-element.37.norm, f32[16,16384]{1,0:T(8,128)} %old_hbm.1), custom_call_target="tpu_custom_call" | custom-call | tf_op jit(solution)/shard_map/images/pallas_call | solution.py:552
  47.2 0.0 copy-start
  47.2 7.2 %adjoint.1 = (f32[16,16384]{1,0:T(8,128)}, f32[16,16384]{1,0:T(8,128)S(1)}, f32[32,16,512]{2,1,0:T(8,128)S(1)}, f32[16,2048]{1,0:T(8,128)}) custom-call(s32[336]{0:T(512)S(1)} %get-tuple-element.33.pair_list, s32[2]{0:T(128)S(1)} %get-tuple-element.34.count, f32[2,256,128]{2,1,0:T(8,128)S(1)} %get-tuple-element.35.places, ...), custom_call_target="tpu_custom_call" | custom-call | tf_op jit(solution)/shard_map/adjoint/pallas_call | solution.py:575
  54.4 13.6 %gamma.1 = (f32[16,16384]{1,0:T(8,128)S(1)}, f32[1,1]{1,0:T(1,128)}) custom-call(f32[32,16,512]{2,1,0:T(8,128)S(1)} %get-tuple-element.50.acc, f32[16,16384]{1,0:T(8,128)S(1)} %get-tuple-element.51.model, f32[128,128]{1,0:T(8,128)S(1)} %get-tuple-element.52.f, f32[8,128]{1,0:T(8,128)S(1)} %get-tuple-element.39.scal), custom_call_target="tpu_custom_call" | custom-call | tf_op jit(solution)/shard_map/gamma/pallas_call | solution.py:598
  68.0 0.0 copy-done
  68.0 1.7 %multiply_add_fusion = f32[16,16384]{1,0:T(8,128)} fusion(f32[16,16384]{1,0:T(8,128)S(1)} %get-tuple-element.53, f32[16,16384]{1,0:T(8,128)S(1)} %copy-done, f32[]{:T(128)} %bitcast.1), kind=kLoop, calls=%fused_computation | loop fusion | flops 524288 | bytes 3145732 | tf_op jit(solution)/shard_map/add | solution.py:609
Async XLA Ops:
  47.2 20.8 %copy-start = (f32[16,16384]{1,0:T(8,128)S(1)}, f32[16,16384]{1,0:T(8,128)}, u32[]{:S(2)}) copy-start(f32[16,16384]{1,0:T(8,128)} %dirn_in.1) | copy-start | bytes 3145732

commit v2 on v1

--- a/solution.py
+++ b/solution.py
@@ -186,8 +186,11 @@
     return jnp.concatenate([block[w, q] for q in range(CBLOCK // 128)], axis=1)
 
 
-def forward_kernel(entries, st, z, v, img, pair_list, count, places, *rest):
-    kept, spare = rest[:UNROLL], rest[UNROLL]
+def forward_kernel(entries_in, st, z, v, img, list_out, places, *rest):
+    kept = rest[:UNROLL]
+    spare, entries, pair_list, in_sem, out_sem = rest[UNROLL:]
+    fetch = pltpu.make_async_copy(entries_in, entries, in_sem)
+    fetch.start()
     slots = st.shape[1]
     pad = jnp.zeros((128 - slots, SBLOCK), F32)
     shift = lax.broadcasted_iota(jnp.int32, (slots, SBLOCK), 0) // entries.shape[1] - REACH
@@ -195,6 +198,9 @@
     places[1] = jnp.concatenate([STRETCH * st[1], pad], axis=0).T
     rows = entries.shape[1]
     img[...] = jnp.zeros(img.shape, F32)
+    last = UNROLL - 1
+    kept[last][0] = jnp.zeros(kept[last].shape[1:], BF16)
+    fetch.wait()
     nothing = SPAN * rows * 32
     pair_list[UNROLL - 1] = nothing
     filled = jnp.int32(UNROLL)
@@ -210,8 +216,10 @@
         pair_list[filled + u] = nothing
     steps = (filled - 1) // UNROLL
     held = jnp.minimum(steps, KEPT // UNROLL)
-    count[0] = steps
-    count[1] = held
+    pair_list[0] = steps
+    pair_list[1] = held
+    leave = pltpu.make_async_copy(pair_list, list_out, out_sem)
+    leave.start()
 
     def multiply(entry, block):
         j = lax.shift_right_logical(entry, 5)
@@ -223,9 +231,6 @@
             )
         img[j] += out[0:16] + out[16:32]
 
-    last = UNROLL - 1
-    kept[last][0] = jnp.zeros(kept[last].shape[1:], BF16)
-
     def step(i, carry):
         at = (i + 1) * UNROLL
         for u in range(UNROLL):
@@ -246,6 +251,7 @@
     lax.fori_loop(0, held, step, 0)
     multiply(pair_list[held * UNROLL + last], kept[last].at[jnp.maximum(held - 1, 0)])
     lax.fori_loop(held, steps, step_over, 0)
+    leave.wait()
 
 
 def all_sum(n, me, mine, landing, send_sem, recv_sem, start, finish):
@@ -400,17 +406,21 @@
     give_sibling.wait()
 
 
-def adjoint_kernel(pair_list, count, places, z, newres, scal, model_in, dirn_in, *rest):
+def adjoint_kernel(list_in, places, z, newres, scal, model_in, dirn_in, *rest):
     kept = rest[:UNROLL]
-    model_hbm, model_o, acc, res_o, dirn, parts, spare, in_sem, out_sem = rest[UNROLL:]
+    model_hbm, model_o, acc, res_hbm, pair_list, res_o, dirn, parts, spare, in_sem, out_sem = rest[UNROLL:]
     slots = newres.shape[0]
     rows = slots // SPAN
     fetch_model = pltpu.make_async_copy(model_in, model_o, in_sem.at[0])
     fetch_dirn = pltpu.make_async_copy(dirn_in, dirn, in_sem.at[1])
+    fetch_list = pltpu.make_async_copy(list_in, pair_list, in_sem.at[2])
+    fetch_list.start()
     fetch_model.start()
     fetch_dirn.start()
     for k in range(rows):
         res_o[:, k * SBLOCK : (k + 1) * SBLOCK] = newres[REACH * rows + k]
+    leave_res = pltpu.make_async_copy(res_o, res_hbm, out_sem.at[1])
+    leave_res.start()
 
     def cut(k, c):
         high, low = split(newres[k])
@@ -439,7 +449,10 @@
             add_pair(j, b, spare)
         return carry
 
-    first = jnp.minimum(count[1], 1)
+    fetch_list.wait()
+    steps = pair_list[0]
+    held = pair_list[1]
+    first = jnp.minimum(held, 1)
     lax.fori_loop(0, first, reread, 0)
     fetch_model.wait()
     fetch_dirn.wait()
@@ -450,10 +463,11 @@
         model_o[:, lanes] = model_o[:, lanes] + length * dirn[:, lanes]
         return c
     lax.fori_loop(0, acc.shape[0], update, 0)
-    leave = pltpu.make_async_copy(model_o, model_hbm, out_sem)
+    leave = pltpu.make_async_copy(model_o, model_hbm, out_sem.at[0])
     leave.start()
-    lax.fori_loop(first, count[1], reread, 0)
-    lax.fori_loop(count[1], count[0], rebuild, 0)
+    lax.fori_loop(first, held, reread, 0)
+    lax.fori_loop(held, steps, rebuild, 0)
+    leave_res.wait()
     leave.wait()
 
 
@@ -492,6 +506,7 @@
     hbm = pl.BlockSpec(memory_space=pltpu.HBM)
     shape = jax.ShapeDtypeStruct
     slots = SPAN * rows
+    listed = slots * pairs + 2 * UNROLL
     one_block = (2, CBLOCK // 128, SBLOCK, 128)
     dma = pltpu.SemaphoreType.DMA
 
@@ -533,17 +548,22 @@
         in_hbm(depth_band.reshape(cells // 128, 128)), in_hbm(station_offsets),
     )
 
-    img, pair_list, count, places, *kept = pl.pallas_call(
+    img, pair_list, places, *kept = pl.pallas_call(
         forward_kernel,
         out_shape=(
             shape((slots + 1, epochs, SBLOCK), F32),
-            shape((slots * pairs + 2 * UNROLL,), jnp.int32),
-            shape((2,), jnp.int32),
+            shape((listed,), jnp.int32),
             shape((2, SBLOCK, 128), F32),
         ) + (pltpu.VMEM((KEPT // UNROLL,) + one_block, BF16),) * UNROLL,
-        in_specs=[smem, vmem, vmem, vmem],
-        out_specs=(vmem, smem, smem) + (vmem,) * (1 + UNROLL),
-        scratch_shapes=[pltpu.VMEM(one_block, BF16)],
+        in_specs=[vmem] * 4,
+        out_specs=(vmem, hbm) + (vmem,) * (1 + UNROLL),
+        scratch_shapes=[
+            pltpu.VMEM(one_block, BF16),
+            pltpu.SMEM((SPAN, rows, pairs), jnp.int32),
+            pltpu.SMEM((listed,), jnp.int32),
+            dma(()),
+            dma(()),
+        ],
         compiler_params=params(),
         name="forward",
     )(entries, st, z, v)
@@ -580,19 +600,21 @@
             shape((blocks, epochs, CBLOCK), F32),
             shape((epochs, stations), F32),
         ),
-        in_specs=[smem, smem] + [vmem] * 4 + [hbm] * 2 + [vmem] * UNROLL,
-        out_specs=(hbm,) + (vmem,) * 3,
+        in_specs=[pl.BlockSpec(memory_space=pl.ANY)] + [vmem] * 4 + [hbm] * 2 + [vmem] * UNROLL,
+        out_specs=(hbm, vmem, vmem, hbm),
         scratch_shapes=[
+            pltpu.SMEM((listed,), jnp.int32),
+            pltpu.VMEM((epochs, stations), F32),
             pltpu.VMEM((epochs, cells), F32),
             pltpu.VMEM((slots + 1, 2 * epochs, SBLOCK), BF16),
             pltpu.VMEM(one_block, BF16),
+            dma((3,)),
             dma((2,)),
-            dma(()),
         ],
         compiler_params=params(),
         name="adjoint",
     )(
-        pair_list, count, places, z, newres, scal, in_hbm(model_field), in_hbm(direction), *kept
+        pair_list, places, z, newres, scal, in_hbm(model_field), in_hbm(direction), *kept
     )
 
     gradient, ratio = pl.pallas_call(

time: 69 us -> 66.8 us (0.968); the launches traced: 69.7 us -> 66.3 us
  Pallas kernels: 67.3 us -> 64 us
    pallas_call x1, Pallas kernels: 29.2 us -> 26.4 us  [shards(): pl.pallas_call(functools.partial(image_kernel, n, rows), out_shape=(shape...]
    pallas_call x1, Pallas kernels: 13.6 us -> 12.4 us  [shards(): pl.pallas_call(functools.partial(gamma_kernel, n), out_shape=(shape((epoc...]
    pallas_call x1, Pallas kernels: 10.8 us -> 11.8 us  [shards(): pl.pallas_call(forward_kernel, out_shape=(shape((slots + 1, epochs, SBLOC...]
where the time goes in v2:
time: 66.8 us; the launch traced here: 66.3 us
  Pallas kernels  64 us (96%)
  other arithmetic  1.68 us (3%)
  between operations  0.69 us (1%)
    pallas_call x1, Pallas kernels, shards(): pl.pallas_call(functools.partial(image_kernel, n, rows), out_shape=(shape...  26.4 us
    pallas_call x1, Pallas kernels, shards(): pl.pallas_call(functools.partial(gamma_kernel, n), out_shape=(shape((epoc...  12.4 us
    pallas_call x1, Pallas kernels, shards(): pl.pallas_call(forward_kernel, out_shape=(shape((slots + 1, epochs, SBLOC...  11.8 us
    pallas_call x1, Pallas kernels, shards(): pl.pallas_call(adjoint_kernel, out_shape=(shape((epochs, cells), F32), sh...  6.86 us
    pallas_call x1, Pallas kernels, shards(): pl.pallas_call(functools.partial(exchange_kernel, n, scale, blocks), out_...  6.51 us
    add x1, other arithmetic, shards(): new_direction = gradient + ratio.reshape(()) * direction  1.68 us

profile of v2, /device:TPU:0, one launch (start us, length us, event | category | flops | bytes accessed | tf_op | source)
XLA Modules:
  0.0 66.3 jit_solution(10923285796979213767)
XLA Ops:
  0.6 6.5 %exchange.1 = (f32[2,40,256]{2,1,0:T(8,128)S(1)}, s32[5,8,8]{2,1,0:T(8,128)S(1)}, bf16[32,32,512]{2,1,0:T(8,128)(2,1)S(1)}, f32[128,128]{1,0:T(8,128)S(1)}, f32[...) custom-call(f32[16,16384]{1,0:T(8,128)} %dirn_in.1, s32[8,8]{1,0:T(8,128)} %pairs.1, s32[128,128]{1,0:T(8,128)} %bitcast.2, ...), custom_call_target="tpu_custom_call" | custom-call | tf_op jit(solution)/shard_map/exchange/pallas_call | solution.py:523
  7.1 11.8 %forward.1 = (f32[41,16,256]{2,1,0:T(8,128)S(1)}, s32[336]{0:T(512)S(1)}, f32[2,256,128]{2,1,0:T(8,128)S(1)}, bf16[11,2,4,256,128]{4,3,2,1,0:T(8,128)(2,1)S(1)},...) custom-call(s32[5,8,8]{2,1,0:T(8,128)S(1)} %get-tuple-element.28.ent, ...), custom_call_target="tpu_custom_call" | custom-call | tf_op jit(solution)/shard_map/forward/pallas_call | solution.py:551
  18.9 26.4 %images.1 = (f32[40,16,256]{2,1,0:T(8,128)S(1)}, f32[8,128]{1,0:T(8,128)S(1)}) custom-call(f32[41,16,256]{2,1,0:T(8,128)S(1)} %get-tuple-element.34.img, f32[16,2048]{1,0:T(8,128)} %res_hbm.1, f32[8,128]{1,0:T(8,128)S(1)} %get-tuple-element.35.norm, f32[16,16384]{1,0:T(8,128)} %old_hbm.1), custom_call_target="tpu_custom_call" | custom-call | tf_op jit(solution)/shard_map/images/pallas_call | solution.py:572
  45.3 0.0 copy-start
  45.4 6.9 %adjoint.1 = (f32[16,16384]{1,0:T(8,128)}, f32[16,16384]{1,0:T(8,128)S(1)}, f32[32,16,512]{2,1,0:T(8,128)S(1)}, f32[16,2048]{1,0:T(8,128)}) custom-call(s32[336]{0:T(512)S(1)} %get-tuple-element.32.list_in, f32[2,256,128]{2,1,0:T(8,128)S(1)} %get-tuple-element.33.places, f32[128,128]{1,0:T(8,128)S(1)} %get-tuple-element.30.z, ...), custom_call_target="tpu_custom_call" | custom-call | tf_op jit(solution)/shard_map/adjoint/pallas_call | solution.py:595
  52.2 12.4 %gamma.1 = (f32[16,16384]{1,0:T(8,128)S(1)}, f32[1,1]{1,0:T(1,128)}) custom-call(f32[32,16,512]{2,1,0:T(8,128)S(1)} %get-tuple-element.48.acc, f32[16,16384]{1,0:T(8,128)S(1)} %get-tuple-element.49.model, f32[128,128]{1,0:T(8,128)S(1)} %get-tuple-element.50.f, f32[8,128]{1,0:T(8,128)S(1)} %get-tuple-element.37.scal), custom_call_target="tpu_custom_call" | custom-call | tf_op jit(solution)/shard_map/gamma/pallas_call | solution.py:620
  64.6 0.0 copy-done
  64.6 1.7 %multiply_add_fusion = f32[16,16384]{1,0:T(8,128)} fusion(f32[16,16384]{1,0:T(8,128)S(1)} %get-tuple-element.51, f32[16,16384]{1,0:T(8,128)S(1)} %copy-done, f32[]{:T(128)} %bitcast.1), kind=kLoop, calls=%fused_computation | loop fusion | flops 524288 | bytes 3145732 | tf_op jit(solution)/shard_map/add | solution.py:631
Async XLA Ops:
  45.3 19.3 %copy-start = (f32[16,16384]{1,0:T(8,128)S(1)}, f32[16,16384]{1,0:T(8,128)}, u32[]{:S(2)}) copy-start(f32[16,16384]{1,0:T(8,128)} %dirn_in.1) | copy-start | bytes 3145732

commit v3 on v2

--- a/solution.py
+++ b/solution.py
@@ -23,12 +23,23 @@
 HOPS = tuple(r for r in range(-REACH, REACH + 1) if r != 0)
 UNROLL = 8
 KEPT = 88
+LAG = 2
 STRIP = 64
 STRETCH = 4.0
 MESH = pl.DeviceIdType.MESH
 F32 = jnp.float32
 BF16 = jnp.bfloat16
 VMEM_LIMIT = 4 * 1024 * 1024
+
+
+def in_groups(size, body, start):
+    group = math.gcd(size, 4)
+
+    def several(k, carry):
+        for m in range(group):
+            carry = body(k * group + m, carry)
+        return carry
+    return lax.fori_loop(0, size // group, several, start)
 
 
 def exists(me, r, n):
@@ -117,7 +128,8 @@
     q = lax.bitwise_and(lax.broadcasted_iota(jnp.int32, z_o.shape, 0), 3).astype(F32)
     z_o[...] = (STRETCH * STRETCH) * (depth * depth) + 0.25 * (q * q)
 
-    def block(b, total):
+    def block(first, b, total):
+        b = first + b
         for q in range(CBLOCK // 128):
             lanes = pl.ds(pl.multiple_of(b * CBLOCK + q * 128, 128), 128)
             values = dirn[:, lanes]
@@ -130,7 +142,7 @@
     total = jnp.zeros((dirn.shape[0], 128), F32)
     for k in range(CHUNKS):
         fetch_dirn[k].wait()
-        total = lax.fori_loop(k * blocks // CHUNKS, (k + 1) * blocks // CHUNKS, block, total)
+        total = in_groups(blocks // CHUNKS, functools.partial(block, k * blocks // CHUNKS), total)
     norm_o[...] = jnp.broadcast_to(lane_sums(total), norm_o.shape)
 
     for q, r in enumerate(HOPS):
@@ -198,11 +210,12 @@
     places[1] = jnp.concatenate([STRETCH * st[1], pad], axis=0).T
     rows = entries.shape[1]
     img[...] = jnp.zeros(img.shape, F32)
-    last = UNROLL - 1
-    kept[last][0] = jnp.zeros(kept[last].shape[1:], BF16)
+    for u in range(UNROLL - LAG, UNROLL):
+        kept[u][0] = jnp.zeros(kept[u].shape[1:], BF16)
     fetch.wait()
     nothing = SPAN * rows * 32
-    pair_list[UNROLL - 1] = nothing
+    for u in range(UNROLL - LAG, UNROLL):
+        pair_list[u] = nothing
     filled = jnp.int32(UNROLL)
     for t in range(SPAN):
         def pick(row, filled):
@@ -235,10 +248,11 @@
         at = (i + 1) * UNROLL
         for u in range(UNROLL):
             fill_block(pair_list[at + u], slots, places, z, kept[u].at[i])
-            if u == 0:
-                multiply(pair_list[at - 1], kept[last].at[jnp.maximum(i - 1, 0)])
+            if u < LAG:
+                earlier = kept[UNROLL + u - LAG].at[jnp.maximum(i - 1, 0)]
             else:
-                multiply(pair_list[at + u - 1], kept[u - 1].at[i])
+                earlier = kept[u - LAG].at[i]
+            multiply(pair_list[at + u - LAG], earlier)
         return carry
 
     def step_over(i, carry):
@@ -249,7 +263,8 @@
         return carry
 
     lax.fori_loop(0, held, step, 0)
-    multiply(pair_list[held * UNROLL + last], kept[last].at[jnp.maximum(held - 1, 0)])
+    for u in range(UNROLL - LAG, UNROLL):
+        multiply(pair_list[held * UNROLL + u], kept[u].at[jnp.maximum(held - 1, 0)])
     lax.fori_loop(held, steps, step_over, 0)
     leave.wait()
 
@@ -336,7 +351,7 @@
 
     fetch_old.wait()
     fetch_res.wait()
-    before = lax.fori_loop(0, old.shape[1] // 512, squares, jnp.zeros((old.shape[0], 512), F32))
+    before = in_groups(old.shape[1] // 512, squares, jnp.zeros((old.shape[0], 512), F32))
     lane = lax.broadcasted_iota(jnp.int32, (1, 128), 1)
     gamma_part = jnp.sum(lane_sums(before), axis=1, keepdims=True)
     norm_part = DAMPING * jnp.sum(norm[0:1, :], axis=1, keepdims=True)
@@ -427,7 +442,7 @@
         parts[k, 0:16, :] = high
         parts[k, 16:32, :] = low
         return c
-    lax.fori_loop(0, slots, cut, 0)
+    in_groups(slots, cut, 0)
     parts[slots] = jnp.zeros((32, SBLOCK), BF16)
     acc[...] = jnp.zeros(acc.shape, F32)
 
@@ -462,7 +477,7 @@
         lanes = pl.ds(pl.multiple_of(b * CBLOCK, CBLOCK), CBLOCK)
         model_o[:, lanes] = model_o[:, lanes] + length * dirn[:, lanes]
         return c
-    lax.fori_loop(0, acc.shape[0], update, 0)
+    in_groups(acc.shape[0], update, 0)
     leave = pltpu.make_async_copy(model_o, model_hbm, out_sem.at[0])
     leave.start()
     lax.fori_loop(first, held, reread, 0)
@@ -484,7 +499,7 @@
         grad_o[:, lanes] = gradient
         return total + gradient * gradient
 
-    total = lax.fori_loop(0, acc.shape[0], finish, jnp.zeros((model.shape[0], CBLOCK), F32))
+    total = in_groups(acc.shape[0], finish, jnp.zeros((model.shape[0], CBLOCK), F32))
     mine[...] = lane_sums(total)
     greeted(n)
     all_sum(n, me, mine, landing, send_sem, recv_sem, True, True)

time: 66.8 us -> 65.3 us (0.978)
  Pallas kernels: 64 us -> 62.8 us
    pallas_call x1, Pallas kernels: 26.4 us -> 28.2 us  [shards(): pl.pallas_call(functools.partial(image_kernel, n, rows), out_shape=(shape...]
    pallas_call x1, Pallas kernels: 11.8 us -> 10.1 us  [shards(): pl.pallas_call(forward_kernel, out_shape=(shape((slots + 1, epochs, SBLOC...]
    pallas_call x1, Pallas kernels: 6.86 us -> 5.25 us  [shards(): pl.pallas_call(adjoint_kernel, out_shape=(shape((epochs, cells), F32), sh...]
where the time goes in v3:
time: 65.3 us; the launch traced here: 65.2 us
  Pallas kernels  62.8 us (96%)
  other arithmetic  1.68 us (3%)
  between operations  0.69 us (1%)
    pallas_call x1, Pallas kernels, shards(): pl.pallas_call(functools.partial(image_kernel, n, rows), out_shape=(shape...  28.2 us
    pallas_call x1, Pallas kernels, shards(): pl.pallas_call(functools.partial(gamma_kernel, n), out_shape=(shape((epoc...  12.7 us
    pallas_call x1, Pallas kernels, shards(): pl.pallas_call(forward_kernel, out_shape=(shape((slots + 1, epochs, SBLOC...  10.1 us
    pallas_call x1, Pallas kernels, shards(): pl.pallas_call(functools.partial(exchange_kernel, n, scale, blocks), out_...  6.51 us
    pallas_call x1, Pallas kernels, shards(): pl.pallas_call(adjoint_kernel, out_shape=(shape((epochs, cells), F32), sh...  5.25 us
    add x1, other arithmetic, shards(): new_direction = gradient + ratio.reshape(()) * direction  1.68 us

profile of v3, /device:TPU:0, one launch (start us, length us, event | category | flops | bytes accessed | tf_op | source)
XLA Modules:
  0.0 65.2 jit_solution(11777691472598255007)
XLA Ops:
  0.6 6.5 %exchange.1 = (f32[2,40,256]{2,1,0:T(8,128)S(1)}, s32[5,8,8]{2,1,0:T(8,128)S(1)}, bf16[32,32,512]{2,1,0:T(8,128)(2,1)S(1)}, f32[128,128]{1,0:T(8,128)S(1)}, f32[...) custom-call(f32[16,16384]{1,0:T(8,128)} %dirn_in.1, s32[8,8]{1,0:T(8,128)} %pairs.1, s32[128,128]{1,0:T(8,128)} %bitcast.2, ...), custom_call_target="tpu_custom_call" | custom-call | tf_op jit(solution)/shard_map/exchange/pallas_call | solution.py:538
  7.1 10.1 %forward.1 = (f32[41,16,256]{2,1,0:T(8,128)S(1)}, s32[336]{0:T(512)S(1)}, f32[2,256,128]{2,1,0:T(8,128)S(1)}, bf16[11,2,4,256,128]{4,3,2,1,0:T(8,128)(2,1)S(1)},...) custom-call(s32[5,8,8]{2,1,0:T(8,128)S(1)} %get-tuple-element.28.ent, ...), custom_call_target="tpu_custom_call" | custom-call | tf_op jit(solution)/shard_map/forward/pallas_call | solution.py:566
  17.3 28.2 %images.1 = (f32[40,16,256]{2,1,0:T(8,128)S(1)}, f32[8,128]{1,0:T(8,128)S(1)}) custom-call(f32[41,16,256]{2,1,0:T(8,128)S(1)} %get-tuple-element.34.img, f32[16,2048]{1,0:T(8,128)} %res_hbm.1, f32[8,128]{1,0:T(8,128)S(1)} %get-tuple-element.35.norm, f32[16,16384]{1,0:T(8,128)} %old_hbm.1), custom_call_target="tpu_custom_call" | custom-call | tf_op jit(solution)/shard_map/images/pallas_call | solution.py:587
  45.5 0.0 copy-start
  45.5 5.2 %adjoint.1 = (f32[16,16384]{1,0:T(8,128)}, f32[16,16384]{1,0:T(8,128)S(1)}, f32[32,16,512]{2,1,0:T(8,128)S(1)}, f32[16,2048]{1,0:T(8,128)}) custom-call(s32[336]{0:T(512)S(1)} %get-tuple-element.32.list_in, f32[2,256,128]{2,1,0:T(8,128)S(1)} %get-tuple-element.33.places, f32[128,128]{1,0:T(8,128)S(1)} %get-tuple-element.30.z, ...), custom_call_target="tpu_custom_call" | custom-call | tf_op jit(solution)/shard_map/adjoint/pallas_call | solution.py:610
  50.8 12.7 %gamma.1 = (f32[16,16384]{1,0:T(8,128)S(1)}, f32[1,1]{1,0:T(1,128)}) custom-call(f32[32,16,512]{2,1,0:T(8,128)S(1)} %get-tuple-element.48.acc, f32[16,16384]{1,0:T(8,128)S(1)} %get-tuple-element.49.model, f32[128,128]{1,0:T(8,128)S(1)} %get-tuple-element.50.f, f32[8,128]{1,0:T(8,128)S(1)} %get-tuple-element.37.scal), custom_call_target="tpu_custom_call" | custom-call | tf_op jit(solution)/shard_map/gamma/pallas_call | solution.py:635
  63.5 0.0 copy-done
  63.5 1.7 %multiply_add_fusion = f32[16,16384]{1,0:T(8,128)} fusion(f32[16,16384]{1,0:T(8,128)S(1)} %get-tuple-element.51, f32[16,16384]{1,0:T(8,128)S(1)} %copy-done, f32[]{:T(128)} %bitcast.1), kind=kLoop, calls=%fused_computation | loop fusion | flops 524288 | bytes 3145732 | tf_op jit(solution)/shard_map/add | solution.py:646
Async XLA Ops:
  45.5 18.0 %copy-start = (f32[16,16384]{1,0:T(8,128)S(1)}, f32[16,16384]{1,0:T(8,128)}, u32[]{:S(2)}) copy-start(f32[16,16384]{1,0:T(8,128)} %dirn_in.1) | copy-start | bytes 3145732
